TPU v7x, 32 devices: a whole 2x2x4 slice. The times are simulated.
32 devices in a mesh: groups: 2 (over y), locus: 4 (over z), design: 2 (over x), chan: 2 (over core).
Axes of the slice: x: 2, y: 2, z: 4, core: 2. Of those that a mesh axis runs over, the one named last changes fastest.
Arguments:
- base_seq: bfloat16 [4, 2048, 128], P(('groups', 'design'), 'locus'), parts along dimension 0, may hold values from -6 to 6
- deltas: bfloat16 [2048, 512], P(('groups', 'locus', 'design')), parts along dimension 0, may hold values from -6 to 6
- owners: int32 [2048, 1], P(('groups', 'locus', 'design')), parts along dimension 0, may hold values from 0 to 7; in each aligned block of 128 rows (0 to 127, 128 to 255, ...) at most 32 rows name the same one
- slot_ids: int32 [2048], P(('groups', 'locus', 'design')), parts along dimension 0, may hold values from 0 to 127
- stem_weight: bfloat16 [128, 1536], P(None, 'chan'), may hold values from -0.5 to 0.5
- dilated_tap_weight: bfloat16 [3, 1536, 768], P(None, None, 'chan'), may hold values from -0.09375 to 0.09375
- mix_weight: bfloat16 [768, 1536], P('chan'), may hold values from -0.21875 to 0.21875
- head_weight: bfloat16 [1536], replicated, may hold values from -5 to 5
Outputs:
- window_grad: float32 [2048, 512], P(('groups', 'locus', 'design')), parts along dimension 0
There are 2 independent parts, one for each index of `groups`. A program takes and returns all parts, laid end to end along the dimension named above; an argument that names none is the same for every part. Nothing has to cross between parts.
Inputs may be any that keep to these rules, and one draw needn't show every extreme that they name: `owners`: owner o stands for bins of segment o // 2 of locus o % 2. Among the 128 windows of one device no owner is named more than 32 times, a bound that some block reaches. `slot_ids`: several windows may name the same target; their changes add.
All inputs are finite; a program needn't handle non-finite values.
Results may differ from a plain program's by a relative error of at most 0.0055.
Values may be sent and summed in bfloat16 or wider, within the bound.
A program may use at most 64 MiB of HBM per device.

v0:
```python
import jax
import jax.numpy as jnp
from jax import lax
from jax.sharding import PartitionSpec as P

DILATION_STEP = 32


def with_halo(cells, sides, width):
    for axis, dim in sides:
        count = lax.axis_size(axis)
        ends = count - 1
        head = lax.slice_in_dim(cells, 0, width, axis=dim)
        tail = lax.slice_in_dim(cells, cells.shape[dim] - width, cells.shape[dim], axis=dim)
        cells = jnp.concatenate(
            [
                lax.ppermute(tail, axis, [(i, (i + 1) % count) for i in range(ends)]),
                cells,
                lax.ppermute(head, axis, [((i + 1) % count, i) for i in range(ends)]),
            ],
            axis=dim,
        )
    return cells


def silu_slope(pre_value):
    sigmoid_value = jax.nn.sigmoid(pre_value)
    return sigmoid_value * (1.0 + pre_value * (1.0 - sigmoid_value))


def gelu_pull(pre_act, cotangent):
    return jax.vjp(lambda argument: jax.nn.gelu(argument, approximate=True), pre_act)[1](cotangent)[
        0
    ]


def stem_back(pulled, weight):
    upper = pulled.astype(jnp.bfloat16)
    lower = (pulled - upper.astype(jnp.float32)).astype(jnp.bfloat16)
    dims = (((1,), (1,)), ((), ()))
    first = lax.dot_general(upper, weight, dims, preferred_element_type=jnp.float32)
    return first + lax.dot_general(lower, weight, dims, preferred_element_type=jnp.float32)


def shards(
    base_seq, deltas, owners, slot_ids, stem_weight, dilated_tap_weight, mix_weight, head_weight
):
    win_dev, row_width = deltas.shape
    bins_per_device, feat_width = (base_seq.shape[1], base_seq.shape[2])
    slots_dev = bins_per_device * feat_width // row_width
    peer_count = lax.axis_size(("locus", "design"))
    capacity = max(2, 2 * win_dev // peer_count)
    bucket_rows = peer_count * capacity
    target_dev = owners[:, 0]
    member = (target_dev[:, None] == jnp.arange(peer_count, dtype=jnp.int32)[None, :]).astype(
        jnp.int32
    )
    earlier = jnp.cumsum(member, axis=0) - member
    bucket_rank = jnp.sum(earlier * member, axis=1)
    position = target_dev * capacity + bucket_rank
    placer = position[None, :] == jnp.arange(bucket_rows, dtype=jnp.int32)[:, None]
    send_rows = jnp.dot(
        placer.astype(jnp.bfloat16), deltas, preferred_element_type=jnp.float32
    ).astype(jnp.bfloat16)
    send_slots = jnp.sum(jnp.where(placer, slot_ids[None, :], 0), axis=1)
    recv_rows, recv_slots = (
        lax.all_to_all(send_rows, ("locus", "design"), split_axis=0, concat_axis=0, tiled=True),
        lax.all_to_all(send_slots, ("locus", "design"), split_axis=0, concat_axis=0, tiled=True),
    )
    chooser = recv_slots[:, None] == jnp.arange(slots_dev, dtype=jnp.int32)[None, :]
    edit_sum = lax.dot_general(
        chooser.astype(jnp.bfloat16),
        recv_rows,
        (((0,), (0,)), ((), ())),
        preferred_element_type=jnp.float32,
    )
    sequence_onehot = (
        base_seq[0].astype(jnp.float32) + edit_sum.reshape(bins_per_device, feat_width)
    ).astype(jnp.bfloat16)
    padded_sequence = with_halo(sequence_onehot, (("locus", 0),), DILATION_STEP)
    stem_full = lax.all_gather(stem_weight, "chan", axis=1, tiled=True)
    gathered_preactivation = jnp.dot(padded_sequence, stem_full, preferred_element_type=jnp.float32)
    hidden_state = jax.nn.gelu(gathered_preactivation, approximate=True).astype(jnp.bfloat16)
    own_width = dilated_tap_weight.shape[2]
    convolved_output = jnp.zeros((bins_per_device, own_width), jnp.float32)
    for filter_tap in range(3):
        convolved_output = convolved_output + jnp.dot(
            hidden_state[filter_tap * DILATION_STEP : filter_tap * DILATION_STEP + bins_per_device],
            dilated_tap_weight[filter_tap],
            preferred_element_type=jnp.float32,
        )
    mix_grad = jnp.dot(mix_weight, head_weight, preferred_element_type=jnp.float32)
    residual_branch = (silu_slope(convolved_output) * mix_grad[None, :]).astype(jnp.bfloat16)
    padded_gradient = with_halo(residual_branch, (("locus", 0),), DILATION_STEP)
    part_sum = jnp.zeros((bins_per_device, stem_full.shape[1]), jnp.float32)
    for filter_tap in range(3):
        lower_boundary = (2 - filter_tap) * DILATION_STEP
        part_sum = part_sum + lax.dot_general(
            padded_gradient[lower_boundary : lower_boundary + bins_per_device],
            dilated_tap_weight[filter_tap],
            (((1,), (1,)), ((), ())),
            preferred_element_type=jnp.float32,
        )
    local_preactivation = gathered_preactivation[DILATION_STEP : DILATION_STEP + bins_per_device]
    summed = lax.psum(part_sum, "chan")
    hidden_grad = head_weight.astype(jnp.float32)[None, :] + summed
    pulled = gelu_pull(local_preactivation, hidden_grad)
    seq_grad = stem_back(pulled, stem_full)
    slot_grad = seq_grad.reshape(slots_dev, row_width)
    back_rows = jnp.dot(chooser.astype(jnp.float32), slot_grad, precision=lax.Precision.HIGHEST)
    returned = lax.all_to_all(
        back_rows, ("locus", "design"), split_axis=0, concat_axis=0, tiled=True
    )
    return lax.dot_general(
        placer.astype(jnp.float32),
        returned,
        (((0,), (0,)), ((), ())),
        precision=lax.Precision.HIGHEST,
    )


def solution(mesh):
    placed = (
        P(("groups", "design"), "locus", None),
        P(("groups", "locus", "design"), None),
        P(("groups", "locus", "design"), None),
        P(("groups", "locus", "design")),
        P(None, "chan"),
        P(None, None, "chan"),
        P("chan", None),
        P(),
    )
    return jax.shard_map(
        shards,
        mesh=mesh,
        in_specs=placed,
        out_specs=P(("groups", "locus", "design"), None),
        check_vma=False,
    )
```

profile of v0, /device:TPU:0, one launch (start us, length us, event | category | flops | bytes accessed | tf_op | source)
XLA Modules:
  0.0 118.4 jit_solution(7377365366886210995)
XLA Ops:
  6.5 0.0 copy-start
  6.5 0.0 copy-start.3
  6.5 0.0 copy-start.2
  6.5 0.8 fusion.66
  7.4 0.2 reduce_window_sum.11
  7.6 0.8 select_reduce_fusion.1
  8.4 0.7 multiply_add_fusion
  9.1 0.8 select_reduce_fusion
  9.8 0.7 all_to_all.22
  10.5 7.3 %all-to-all-start = ((s32[8,32,1]{1,2,0:T(1,128)}), s32[8,32,1]{1,2,0:T(1,128)S(1)}, u32[]{:S(2)}, u32[]{:S(2)}) async-start(s32[8,32,1]{1,2,0:T(1,128)} %all_to_all.22), calls=%async_computation | async-start | bytes 8192 | tf_op jit(solution)/shard_map/all_to_all | solution.py:68
  17.8 1.8 %convolution_convert_fusion = bf16[256,512]{1,0:T(8,128)(2,1)} fusion(bf16[128,512]{1,0:T(8,128)(2,1)} %param.9, s32[128]{0:T(128)S(1)} %multiply_add_fusion), kind=kOutput, calls=%fused_computation.29 | convolution fusion | flops 33718272 | bytes 393728 | tf_op jit(solution)/shard_map/dot_general | solution.py:62
  19.6 4.6 %all-to-all-done = s32[8,32,1]{1,2,0:T(1,128)S(1)} async-done(((s32[8,32,1]{1,2,0:T(1,128)}), s32[8,32,1]{1,2,0:T(1,128)S(1)}, u32[]{:S(2)}, u32[]{:S(2)}) %all-to-all-start) | async-done | bytes 1056 | tf_op jit(solution)/shard_map/all_to_all | solution.py:68
  24.2 3.4 %all-to-all-start.1 = ((bf16[8,32,512]{2,1,0:T(8,128)(2,1)}), bf16[8,32,512]{2,1,0:T(8,128)(2,1)S(1)}, u32[]{:S(2)}, u32[]{:S(2)}) async-start(bf16[8,32,512]{2,1,0:T(8,128)(2,1)} %bitcast.4), calls=%async_computation.1 | async-start | bytes 524288 | tf_op jit(solution)/shard_map/all_to_all | solution.py:67
  27.6 0.0 all-reduce.2.cloned.1.call-start
  27.7 0.7 reshape.52
  28.4 0.0 copy-done
  28.4 0.5 convolution_reduce_fusion
  28.9 0.5 broadcast.62
  29.4 0.6 reduce.5
  30.1 0.1 eq.73
  30.1 5.7 %all-to-all-done.1 = bf16[8,32,512]{2,1,0:T(8,128)(2,1)S(1)} async-done(((bf16[8,32,512]{2,1,0:T(8,128)(2,1)}), bf16[8,32,512]{2,1,0:T(8,128)(2,1)S(1)}, u32[]{:S(2)}, u32[]{:S(2)}) %all-to-all-start.1) | async-done | bytes 262176 | tf_op jit(solution)/shard_map/all_to_all | solution.py:67
  35.8 0.3 fusion.61
  36.1 0.0 copy-done.3
  36.2 2.0 %collective-permute-start = (bf16[32,128]{1,0:T(8,128)(2,1)S(1)}, bf16[32,128]{1,0:T(8,128)(2,1)S(1)}, u32[]{:S(2)}, u32[]{:S(2)}) collective-permute-start(bf16[32,128]{1,0:T(8,128)(2,1)S(1)} %get-tuple-element.7), channel_id=1, source_target_pairs={{0,4},{4,8},{8,12},{1,5},{5,9},{9,13},{2,6},{6,10},{10,14},{3,7},{... | collective-permute-start | bytes 24584 | tf_op jit(solution)/shard_map/ppermute | solution.py:17
  38.2 1.3 %collective-permute-start.1 = (bf16[32,128]{1,0:T(8,128)(2,1)S(1)}, bf16[32,128]{1,0:T(8,128)(2,1)S(1)}, u32[]{:S(2)}, u32[]{:S(2)}) collective-permute-start(bf16[32,128]{1,0:T(8,128)(2,1)S(1)} %get-tuple-element.8), channel_id=1, source_target_pairs={{4,0},{8,4},{12,8},{5,1},{9,5},{13,9},{6,2},{10,6},{14,10},{7,3},{... | collective-permute-start | bytes 24584 | tf_op jit(solution)/shard_map/ppermute | solution.py:19
  39.5 0.0 copy-done.2
  39.5 2.1 %all_gather.3 = bf16[128,1536]{1,0:T(8,128)(2,1)S(1)} all-gather(bf16[128,768]{1,0:T(8,128)(2,1)S(1)} %copy-done.2), channel_id=1, replica_groups=mesh['groups'=2,'locus'=4,'design'=2,'chan'=2] {'chan'}, dimensions={1}, use_global_device_ids=true | all-gather | bytes 589824 | tf_op jit(solution)/shard_map/all_gather | solution.py:81
  41.6 0.0 copy-start.1
  41.6 0.0 collective-permute-done
  41.6 2.1 %collective-permute-done.1 = bf16[32,128]{1,0:T(8,128)(2,1)S(1)} collective-permute-done((bf16[32,128]{1,0:T(8,128)(2,1)S(1)}, bf16[32,128]{1,0:T(8,128)(2,1)S(1)}, u32[]{:S(2)}, u32[]{:S(2)}) %collective-permute-start.1) | collective-permute-done | bytes 8224 | tf_op jit(solution)/shard_map/ppermute | solution.py:19
  43.8 2.9 %fusion.7 = (bf16[576,1536]{1,0:T(8,128)(2,1)S(1)}, f32[576,1536]{1,0:T(8,128)}) fusion(bf16[128,1536]{1,0:T(8,128)(2,1)S(1)} %all_gather.3, bf16[32,128]{1,0:T(8,128)(2,1)S(1)} %collective-permute-done.1, bf16[512,128]{1,0:T(8,128)(2,1)S(1)} %fusion.50, bf16[32,128]{1,0:T(8,128)(2,1)S(1)} %collective-permute-done), kind=kOutput, calls=%fused_computation.10 | convolution fusion | flops 234897408 | bytes 5849088 | tf_op jit(solution)/shard_map/dot_general | solution.py:82
  46.7 0.0 copy-done.1
  46.7 1.0 fusion.18
  47.7 1.0 fusion.22
  48.7 1.2 multiply_convert_fusion
  49.9 2.9 %collective-permute-start.3 = (bf16[32,384]{1,0:T(8,128)(2,1)S(1)}, bf16[32,384]{1,0:T(8,128)(2,1)S(1)}, u32[]{:S(2)}, u32[]{:S(2)}) collective-permute-start(bf16[32,384]{1,0:T(8,128)(2,1)S(1)} %get-tuple-element.6), channel_id=1, source_target_pairs={{0,4},{4,8},{8,12},{1,5},{5,9},{9,13},{2,6},{6,10},{10,14},{3,7},{... | collective-permute-start | bytes 73736 | tf_op jit(solution)/shard_map/ppermute | solution.py:17
  52.8 1.0 fusion.31
  53.8 1.3 %collective-permute-start.2 = (bf16[32,384]{1,0:T(8,128)(2,1)S(1)}, bf16[32,384]{1,0:T(8,128)(2,1)S(1)}, u32[]{:S(2)}, u32[]{:S(2)}) collective-permute-start(bf16[32,384]{1,0:T(8,128)(2,1)S(1)} %get-tuple-element.5), channel_id=1, source_target_pairs={{4,0},{8,4},{12,8},{5,1},{9,5},{13,9},{6,2},{10,6},{14,10},{7,3},{... | collective-permute-start | bytes 73736 | tf_op jit(solution)/shard_map/ppermute | solution.py:19
  55.1 0.0 collective-permute-done.3
  55.1 1.0 fusion.28
  56.1 3.4 %collective-permute-done.2 = bf16[32,384]{1,0:T(8,128)(2,1)S(1)} collective-permute-done((bf16[32,384]{1,0:T(8,128)(2,1)S(1)}, bf16[32,384]{1,0:T(8,128)(2,1)S(1)}, u32[]{:S(2)}, u32[]{:S(2)}) %collective-permute-start.2) | collective-permute-done | bytes 24608 | tf_op jit(solution)/shard_map/ppermute | solution.py:19
  59.5 2.8 %fusion.8 = f32[512,1536]{1,0:T(8,128)} fusion(f32[512,1536]{1,0:T(8,128)S(1)} %fusion.28, f32[512,1536]{1,0:T(8,128)S(1)} %fusion.31, bf16[3,1536,384]{2,1,0:T(8,128)(2,1)S(1)} %copy-done.1, bf16[32,384]{1,0:T(8,128)(2,1)S(1)} %collective-permute-done.2, bf16[512,384]{1,0:T(8,128)(2,1)S(1)} %multiply_convert_fusion), kind=kOutput, calls=%fused_computation.12 | convolution fusion | flops 606339072 | bytes 11034624 | tf_op jit(solution)/shard_map/dot_general | solution.py:98
  62.3 0.0 copy-start.4
  62.3 0.0 all-reduce.2.cloned.1.call-update
  62.3 0.7 copy-done.4
  63.0 21.2 %all-reduce.2.cloned.1.call-done = f32[512,1536]{1,0:T(8,128)} async-done(((f32[512,1536]{1,0:T(8,128)}), f32[512,1536]{1,0:T(8,128)}) %all-reduce.2.cloned.1.call-update) | async-done | bytes 3145744 | tf_op jit(solution)/shard_map/psum | solution.py:105
  84.2 4.1 %fusion.14 = f32[512,1536]{1,0:T(8,128)S(1)} fusion(f32[576,1536]{1,0:T(8,128)} %get-tuple-element.10, f32[512,1536]{1,0:T(8,128)} %all-reduce.2.cloned.1.call-done, f32[1536]{0:T(1024)S(1)} %convert_element_type.38), kind=kLoop, calls=%fused_computation.18 | loop fusion | flops 15728640 | bytes 9443328 | tf_op jit(solution)/shard_map/transpose(jvp())/add_any | solution.py:32
  88.3 0.6 fusion.15
  88.9 0.6 convolution_add_fusion.1
  89.5 0.4 fusion.59
  89.9 20.5 %all_to_all.33 = f32[8,32,512]{2,1,0:T(8,128)S(1)} all-to-all(f32[8,32,512]{2,1,0:T(8,128)S(1)} %fusion.59), channel_id=1, replica_groups=mesh['groups'=2,'locus'=4,'design'=2,'chan'=2] {'locus','design'}, dimensions={0} | all-to-all | bytes 1048576 | tf_op jit(solution)/shard_map/all_to_all | solution.py:111
  110.4 1.1 fusion.57
  (6 shorter events, 0.1 us)
Async XLA Ops:
  6.5 21.9 %copy-start = (bf16[384,1536]{1,0:T(8,128)(2,1)S(1)}, bf16[384,1536]{1,0:T(8,128)(2,1)}, u32[]{:S(2)}) copy-start(bf16[384,1536]{1,0:T(8,128)(2,1)} %param.14) | copy-start | bytes 3538948
  6.5 29.6 %copy-start.3 = (bf16[1,512,128]{2,1,0:T(8,128)(2,1)S(1)}, bf16[1,512,128]{2,1,0:T(8,128)(2,1)}, u32[]{:S(2)}) copy-start(bf16[1,512,128]{2,1,0:T(8,128)(2,1)} %param.8) | copy-start | bytes 393220
  6.5 33.0 %copy-start.2 = (bf16[128,768]{1,0:T(8,128)(2,1)S(1)}, bf16[128,768]{1,0:T(8,128)(2,1)}, u32[]{:S(2)}) copy-start(bf16[128,768]{1,0:T(8,128)(2,1)} %param.12) | copy-start | bytes 589828
  10.5 13.7 %all-to-all-start = ((s32[8,32,1]{1,2,0:T(1,128)}), s32[8,32,1]{1,2,0:T(1,128)S(1)}, u32[]{:S(2)}, u32[]{:S(2)}) async-start(s32[8,32,1]{1,2,0:T(1,128)} %all_to_all.22), calls=%async_computation | async-start | bytes 8192 | tf_op jit(solution)/shard_map/all_to_all | solution.py:68
  24.2 11.6 %all-to-all-start.1 = ((bf16[8,32,512]{2,1,0:T(8,128)(2,1)}), bf16[8,32,512]{2,1,0:T(8,128)(2,1)S(1)}, u32[]{:S(2)}, u32[]{:S(2)}) async-start(bf16[8,32,512]{2,1,0:T(8,128)(2,1)} %bitcast.4), calls=%async_computation.1 | async-start | bytes 524288 | tf_op jit(solution)/shard_map/all_to_all | solution.py:67
  27.6 56.6 %all-reduce.2.cloned.1.call-start = ((), (), s32[]{:S(2)}) async-start(), calls=%async_computation.3 | async-start | bytes 6291456 | tf_op jit(solution)/shard_map/psum | solution.py:105
  36.2 5.4 %collective-permute-start = (bf16[32,128]{1,0:T(8,128)(2,1)S(1)}, bf16[32,128]{1,0:T(8,128)(2,1)S(1)}, u32[]{:S(2)}, u32[]{:S(2)}) collective-permute-start(bf16[32,128]{1,0:T(8,128)(2,1)S(1)} %get-tuple-element.7), channel_id=1, source_target_pairs={{0,4},{4,8},{8,12},{1,5},{5,9},{9,13},{2,6},{6,10},{10,14},{3,7},{... | collective-permute-start | bytes 24584 | tf_op jit(solution)/shard_map/ppermute | solution.py:17
  38.2 5.5 %collective-permute-start.1 = (bf16[32,128]{1,0:T(8,128)(2,1)S(1)}, bf16[32,128]{1,0:T(8,128)(2,1)S(1)}, u32[]{:S(2)}, u32[]{:S(2)}) collective-permute-start(bf16[32,128]{1,0:T(8,128)(2,1)S(1)} %get-tuple-element.8), channel_id=1, source_target_pairs={{4,0},{8,4},{12,8},{5,1},{9,5},{13,9},{6,2},{10,6},{14,10},{7,3},{... | collective-permute-start | bytes 24584 | tf_op jit(solution)/shard_map/ppermute | solution.py:19
  41.6 5.1 %copy-start.1 = (bf16[3,1536,384]{2,1,0:T(8,128)(2,1)S(1)}, bf16[3,1536,384]{2,1,0:T(8,128)(2,1)}, u32[]{:S(2)}) copy-start(bf16[3,1536,384]{2,1,0:T(8,128)(2,1)} %param.13) | copy-start | bytes 10616836
  49.9 5.3 %collective-permute-start.3 = (bf16[32,384]{1,0:T(8,128)(2,1)S(1)}, bf16[32,384]{1,0:T(8,128)(2,1)S(1)}, u32[]{:S(2)}, u32[]{:S(2)}) collective-permute-start(bf16[32,384]{1,0:T(8,128)(2,1)S(1)} %get-tuple-element.6), channel_id=1, source_target_pairs={{0,4},{4,8},{8,12},{1,5},{5,9},{9,13},{2,6},{6,10},{10,14},{3,7},{... | collective-permute-start | bytes 73736 | tf_op jit(solution)/shard_map/ppermute | solution.py:17
  53.8 5.7 %collective-permute-start.2 = (bf16[32,384]{1,0:T(8,128)(2,1)S(1)}, bf16[32,384]{1,0:T(8,128)(2,1)S(1)}, u32[]{:S(2)}, u32[]{:S(2)}) collective-permute-start(bf16[32,384]{1,0:T(8,128)(2,1)S(1)} %get-tuple-element.5), channel_id=1, source_target_pairs={{4,0},{8,4},{12,8},{5,1},{9,5},{13,9},{6,2},{10,6},{14,10},{7,3},{... | collective-permute-start | bytes 73736 | tf_op jit(solution)/shard_map/ppermute | solution.py:19
  62.3 0.7 copy-start.4
Sparse Core Ops, SparseCore 0:
  62.4 21.7 all-reduce.1
where the time goes:
time: 119 us; the launch traced here: 118 us
  waiting for transfers between devices  37.1 us (31%)
  blocking collectives  22.6 us (19%)
  starting transfers between devices  18.2 us (15%)
  matrix products  16 us (13%)
  between operations  13.6 us (11%)
  other arithmetic  8.02 us (7%)
  local copies, waits for them, and re-layouts  2.73 us (2%)
    psum x1, waiting for transfers between devices, shards(): summed = lax.psum(part_sum, 'chan')  21.2 us
    all_to_all x1, blocking collectives, shards(): lax.all_to_all(back_rows, ('locus', 'design'), split_axis=0, concat_axis=...  20.5 us
    all_to_all x1, starting transfers between devices, shards(): lax.all_to_all(send_slots, ('locus', 'design'), split_axis=0, concat_axis...  7.25 us
    all_to_all x1, waiting for transfers between devices, shards(): lax.all_to_all(send_rows, ('locus', 'design'), split_axis=0, concat_axis=...  5.68 us
    ppermute x2, waiting for transfers between devices, with_halo(): lax.ppermute(head, axis, [((i + 1) % count, i) for i in range(ends)])  5.54 us
    ppermute x2, starting transfers between devices, with_halo(): lax.ppermute(tail, axis, [(i, (i + 1) % count) for i in range(ends)])  4.95 us
    dot_general x3, matrix products, shards(): lax.dot_general(padded_gradient[lower_boundary:lower_boundary + bins_per_...  4.77 us
    all_to_all x1, waiting for transfers between devices, shards(): lax.all_to_all(send_slots, ('locus', 'design'), split_axis=0, concat_axis...  4.64 us
  transfers between devices with their start and end apart: 7, of which 5 were waited for; matrix products, arithmetic and copies ran while one was open for 5% of the time, Pallas kernels for 0%

commit v1 on v0

--- a/solution.py
+++ b/solution.py
@@ -1,9 +1,15 @@
+import functools
+
 import jax
 import jax.numpy as jnp
 from jax import lax
+from jax.experimental import pallas as pl
+from jax.experimental.pallas import tpu as pltpu
 from jax.sharding import PartitionSpec as P
 
 DILATION_STEP = 32
+MESH = pl.DeviceIdType.MESH
+NT = (((1,), (1,)), ((), ()))
 
 
 def with_halo(cells, sides, width):
@@ -55,7 +61,11 @@
     member = (target_dev[:, None] == jnp.arange(peer_count, dtype=jnp.int32)[None, :]).astype(
         jnp.int32
     )
-    earlier = jnp.cumsum(member, axis=0) - member
+    order = jnp.arange(win_dev, dtype=jnp.int32)
+    before = (order[None, :] < order[:, None]).astype(jnp.bfloat16)
+    earlier = jnp.dot(
+        before, member.astype(jnp.bfloat16), preferred_element_type=jnp.float32
+    ).astype(jnp.int32)
     bucket_rank = jnp.sum(earlier * member, axis=1)
     position = target_dev * capacity + bucket_rank
     placer = position[None, :] == jnp.arange(bucket_rows, dtype=jnp.int32)[:, None]
@@ -119,6 +129,440 @@
     )
 
 
+def dot(left, right):
+    return jnp.dot(left, right, preferred_element_type=jnp.float32)
+
+
+def dot_nt(left, right):
+    return lax.dot_general(left, right, NT, preferred_element_type=jnp.float32)
+
+
+def iota(shape, axis):
+    return lax.broadcasted_iota(jnp.int32, shape, axis)
+
+
+def to_column(row):
+    count = row.shape[1]
+    eye = iota((count, count), 0) == iota((count, count), 1)
+    return jnp.sum(jnp.where(eye, row, 0.0), axis=1, keepdims=True)
+
+
+def gelu_parts(value):
+    square = value * value
+    root = 0.7978845608028654
+    curve = jnp.tanh(value * (root + (root * 0.044715) * square))
+    return square, curve
+
+
+def gelu_value(value):
+    half = 0.5 * value
+    return half + half * gelu_parts(value)[1]
+
+
+def gelu_slope(value):
+    square, curve = gelu_parts(value)
+    root = 0.7978845608028654
+    inner = value * (root + (3.0 * root * 0.044715) * square)
+    return 0.5 * (1.0 + curve) + 0.5 * (1.0 - curve * curve) * inner
+
+
+def kernel(
+    n_locus,
+    n_design,
+    base_ref,
+    deltas_ref,
+    owners_ref,
+    slots_ref,
+    stem_hbm,
+    taps_hbm,
+    mix_hbm,
+    head_ref,
+    out_ref,
+    stem_ref,
+    taps_ref,
+    mix_ref,
+    send_rows,
+    send_slots,
+    recv_rows,
+    recv_slots,
+    seq_ref,
+    hidden_ref,
+    branch_ref,
+    part_send,
+    part_recv,
+    back_ref,
+    ret_ref,
+    half_ref,
+    other_ref,
+    load_sem,
+    rows_sem,
+    slots_sem,
+    stem_sem,
+    seq_sem,
+    halo_sem,
+    part_sem,
+    back_sem,
+    half_sem,
+):
+    group, locus = lax.axis_index("groups"), lax.axis_index("locus")
+    design, core = lax.axis_index("design"), lax.axis_index("chan")
+    peers = n_locus * n_design
+    me = locus * n_design + design
+    wins, width = deltas_ref.shape
+    half_width = width // 2
+    cap = recv_rows.shape[1]
+    stem_half = stem_hbm.shape[1]
+    channels = stem_ref.shape[1]
+    blocks = seq_ref.shape[0] - 4
+    slots = blocks * 8
+    tile = part_send.shape[2]
+    tiles = channels // tile
+    mates = 1 - core
+    partner = (group, locus, design, mates)
+
+    def peer(index):
+        return (group, index // n_design, index % n_design, core)
+
+    own_columns = pl.ds(pl.multiple_of(core * half_width, half_width), half_width)
+    other_columns = pl.ds(pl.multiple_of(mates * half_width, half_width), half_width)
+    own_stem = pl.ds(pl.multiple_of(core * stem_half, stem_half), stem_half)
+
+    load_taps = pltpu.make_async_copy(taps_hbm, taps_ref, load_sem.at[0])
+    load_mix = pltpu.make_async_copy(mix_hbm, mix_ref, load_sem.at[1])
+    load_stem = pltpu.make_async_copy(stem_hbm, stem_ref.at[:, own_stem], load_sem.at[2])
+    load_stem.start()
+    load_mix.start()
+    load_taps.start()
+
+    barrier = pltpu.get_barrier_semaphore()
+
+    def greet(device):
+        pl.semaphore_signal(barrier, inc=1, device_id=device, device_id_type=MESH)
+
+    for step in range(1, peers):
+        greet(peer((me + step) % peers))
+    greet(partner)
+
+    @pl.when(locus > 0)
+    def _():
+        greet((group, locus - 1, design, mates))
+
+    @pl.when(locus < n_locus - 1)
+    def _():
+        greet((group, locus + 1, design, mates))
+
+    bucket_row = owners_ref[...] - me
+    bucket_row = jnp.where(bucket_row < 0, bucket_row + peers, bucket_row)
+    member = (iota((peers, wins), 0) == bucket_row).astype(jnp.float32)
+    before = (iota((wins, wins), 0) < iota((wins, wins), 1)).astype(jnp.bfloat16)
+    earlier = dot(member.astype(jnp.bfloat16), before)
+    rank_row = jnp.sum(earlier * member, axis=0, keepdims=True).astype(jnp.int32)
+    place_row = bucket_row * cap + rank_row
+    placer = (iota((peers * cap, wins), 0) == place_row).astype(jnp.bfloat16)
+    picked = dot(placer, deltas_ref[:, own_columns]).astype(jnp.bfloat16)
+    send_rows[...] = picked.reshape(peers, cap, half_width)
+    lane_row = jnp.bitwise_and(place_row, 127)
+    lanes = (iota((128, wins), 0) == lane_row).astype(jnp.bfloat16)
+    slot_row = slots_ref[...].astype(jnp.float32)
+    slot_table = dot_nt((member * slot_row).astype(jnp.bfloat16), lanes)
+    for step in range(peers):
+        send_slots[step] = jnp.broadcast_to(slot_table[step : step + 1, :], (8, 128))
+
+    callers = peers + jnp.where(locus > 0, 1, 0) + jnp.where(locus < n_locus - 1, 1, 0)
+    pl.semaphore_wait(barrier, callers)
+
+    def remote(source, target, sems, index, device):
+        return pltpu.make_async_remote_copy(
+            src_ref=source,
+            dst_ref=target,
+            send_sem=sems.at[0, index],
+            recv_sem=sems.at[1, index],
+            device_id=device,
+            device_id_type=MESH,
+        )
+
+    row_copies, slot_copies = [], []
+    for step in range(1, peers):
+        device = peer((me + step) % peers)
+        slot_copies.append(
+            remote(send_slots.at[step], recv_slots.at[step], slots_sem, step, device)
+        )
+        row_copies.append(remote(send_rows.at[step], recv_rows.at[step], rows_sem, step, device))
+        slot_copies[-1].start()
+        row_copies[-1].start()
+    stem_copy = remote(stem_hbm, stem_ref.at[:, own_stem], stem_sem, 0, partner)
+    stem_copy.start()
+
+    recv_rows[0] = send_rows[0]
+    recv_slots[0] = send_slots[0]
+    place_column = to_column(place_row.astype(jnp.float32)).astype(jnp.int32)
+
+    @pl.when(locus == 0)
+    def _():
+        seq_ref[0:2] = jnp.zeros((2,) + seq_ref.shape[1:], jnp.bfloat16)
+
+    @pl.when(locus == n_locus - 1)
+    def _():
+        seq_ref[blocks + 2 : blocks + 4] = jnp.zeros((2,) + seq_ref.shape[1:], jnp.bfloat16)
+
+    line = iota((64, 128), 0)
+    wanted = (line // 16) * 32 + (line % 8) * 4 + core * 2 + (line // 8) % 2
+    shuffle = (wanted == iota((64, 128), 1)).astype(jnp.bfloat16)
+    base_own = jnp.concatenate(
+        [dot(shuffle, base_ref[0, 128 * part : 128 * part + 128, :]) for part in range(blocks // 4)],
+        axis=0,
+    )
+    load_mix.wait()
+    head_row = head_ref[...]
+    mix_grad = dot_nt(jnp.broadcast_to(head_row, (16, channels)), mix_ref[...])[0:1, :]
+
+    for copy in slot_copies:
+        copy.wait_recv()
+    per = 128 // cap
+    slot_rows = []
+    for part in range(peers // per):
+        total = recv_slots[part * per]
+        for step in range(part * per + 1, part * per + per):
+            total = total + recv_slots[step]
+        slot_rows.append(total[0:1, :])
+    gathers = [iota((slots, 128), 0) == row.astype(jnp.int32) for row in slot_rows]
+    chooser = jnp.concatenate(
+        [
+            (to_column(row).astype(jnp.int32) == iota((128, slots), 1)).astype(jnp.bfloat16)
+            for row in slot_rows
+        ],
+        axis=0,
+    )
+    for copy in row_copies:
+        copy.wait_recv()
+    edit = jnp.zeros((slots, half_width), jnp.float32)
+    for part, gather in enumerate(gathers):
+        rows = recv_rows[part * per : part * per + per].reshape(128, half_width)
+        edit = edit + dot(gather.astype(jnp.bfloat16), rows)
+    edit_own = jnp.stack(
+        [edit[:, 0:128].reshape(blocks, 8, 128), edit[:, 128:256].reshape(blocks, 8, 128)], axis=1
+    ).reshape(blocks * 16, 128)
+    seq_own = (base_own + edit_own).astype(jnp.bfloat16)
+    seq_ref[pl.ds(2, blocks), core] = seq_own.reshape(blocks, 16, 128)
+
+    mine = seq_ref.at[pl.ds(2, blocks), core]
+    seq_copy = remote(mine, mine, seq_sem, 0, partner)
+    first, last = seq_ref.at[pl.ds(2, 2), core], seq_ref.at[pl.ds(blocks, 2), core]
+    past, ahead = seq_ref.at[pl.ds(0, 2), core], seq_ref.at[pl.ds(blocks + 2, 2), core]
+    up = [
+        remote(last, past, halo_sem, 0, (group, locus + 1, design, core)),
+        remote(last, past, halo_sem, 1, (group, locus + 1, design, mates)),
+    ]
+    down = [
+        remote(first, ahead, halo_sem, 2, (group, locus - 1, design, core)),
+        remote(first, ahead, halo_sem, 3, (group, locus - 1, design, mates)),
+    ]
+
+    @pl.when(locus < n_locus - 1)
+    def _():
+        for copy in up:
+            copy.start()
+
+    @pl.when(locus > 0)
+    def _():
+        for copy in down:
+            copy.start()
+
+    seq_copy.start()
+    load_stem.wait()
+    stem_copy.wait()
+    load_taps.wait()
+    seq_copy.wait()
+
+    @pl.when(locus > 0)
+    def _():
+        for copy in up:
+            copy.wait_recv()
+
+    @pl.when(locus < n_locus - 1)
+    def _():
+        for copy in down:
+            copy.wait_recv()
+
+    rows_all = (blocks + 4) * 32
+    conv_rows = (blocks + 2) * 32
+    seq_all = seq_ref[...].reshape(rows_all, 128)
+    for part in range(tiles):
+        columns = slice(part * tile, part * tile + tile)
+        pre_act = dot(seq_all, stem_ref[:, columns])
+        hidden_ref[:, columns] = gelu_value(pre_act).astype(jnp.bfloat16)
+
+    conv = dot(hidden_ref[0:conv_rows, :], taps_ref[0])
+    for tap in range(1, 3):
+        conv = conv + dot(hidden_ref[32 * tap : 32 * tap + conv_rows, :], taps_ref[tap])
+    branch = (silu_slope(conv) * mix_grad).astype(jnp.bfloat16)
+    branch_ref[...] = branch.reshape(branch_ref.shape)
+
+    @pl.when(locus == 0)
+    def _():
+        branch_ref[0] = jnp.zeros(branch_ref.shape[1:], jnp.bfloat16)
+
+    @pl.when(locus == n_locus - 1)
+    def _():
+        branch_ref[blocks + 1] = jnp.zeros(branch_ref.shape[1:], jnp.bfloat16)
+
+    own_rows = blocks * 16
+
+    def taps_of(side):
+        return [
+            branch_ref[pl.ds(2 - tap, blocks), side].reshape(own_rows, branch_ref.shape[3])
+            for tap in range(3)
+        ]
+
+    def back_tile(inputs, part):
+        lines = slice(part * tile, part * tile + tile)
+        total = dot_nt(inputs[0], taps_ref[0, lines, :])
+        for tap in range(1, 3):
+            total = total + dot_nt(inputs[tap], taps_ref[tap, lines, :])
+        return total
+
+    theirs = taps_of(mates)
+    part_copies = []
+    for part in range(tiles):
+        part_send[part] = back_tile(theirs, part).astype(jnp.bfloat16)
+        part_copies.append(
+            remote(part_send.at[part], part_recv.at[part], part_sem, part, partner)
+        )
+        part_copies[-1].start()
+    ours = taps_of(core)
+    seq_grad = jnp.zeros((own_rows, 128), jnp.float32)
+    for part in range(tiles):
+        columns = slice(part * tile, part * tile + tile)
+        own = back_tile(ours, part) + head_row[:, columns].astype(jnp.float32)
+        slope = gelu_slope(dot(seq_own, stem_ref[:, columns]))
+        part_copies[part].wait_recv()
+        pulled = slope * (own + part_recv[part].astype(jnp.float32))
+        seq_grad = seq_grad + dot_nt(pulled.astype(jnp.bfloat16), stem_ref[:, columns])
+
+    grads = seq_grad.reshape(blocks, 2, 8, 128)
+    slot_grad = jnp.concatenate(
+        [grads[:, 0].reshape(slots, 128), grads[:, 1].reshape(slots, 128)], axis=1
+    ).astype(jnp.bfloat16)
+    back = dot(chooser, slot_grad).astype(jnp.bfloat16)
+    back_ref[...] = back.reshape(back_ref.shape)
+    back_copies = []
+    for step in range(1, peers):
+        device = peer((me + peers - step) % peers)
+        back_copies.append(remote(back_ref.at[step], ret_ref.at[step], back_sem, step, device))
+        back_copies[-1].start()
+    ret_ref[0] = back_ref[0]
+    unplacer = (place_column == iota((wins, peers * cap), 1)).astype(jnp.bfloat16)
+    for copy in back_copies:
+        copy.wait_recv()
+    result = dot(unplacer, ret_ref[...].reshape(peers * cap, half_width))
+    half_ref[...] = result.astype(jnp.bfloat16)
+    half_copy = remote(half_ref, other_ref, half_sem, 0, partner)
+    half_copy.start()
+    out_ref[:, own_columns] = result
+    for copy in slot_copies + row_copies + part_copies + back_copies:
+        copy.wait_send()
+
+    @pl.when(locus < n_locus - 1)
+    def _():
+        for copy in up:
+            copy.wait_send()
+
+    @pl.when(locus > 0)
+    def _():
+        for copy in down:
+            copy.wait_send()
+
+    half_copy.wait()
+    out_ref[:, other_columns] = other_ref[...].astype(jnp.float32)
+
+
+def fused(
+    n_locus,
+    n_design,
+    base_seq,
+    deltas,
+    owners,
+    slot_ids,
+    stem_weight,
+    dilated_tap_weight,
+    mix_weight,
+    head_weight,
+):
+    wins, width = deltas.shape
+    peers = n_locus * n_design
+    cap = 2 * wins // peers
+    blocks = base_seq.shape[1] // DILATION_STEP
+    channels, own_width = dilated_tap_weight.shape[1:]
+    feats = base_seq.shape[2]
+    tile = 256
+    tiles = channels // tile
+    bf16, f32 = jnp.bfloat16, jnp.float32
+    whole = pl.BlockSpec(memory_space=pltpu.VMEM)
+    anywhere = pl.BlockSpec(memory_space=pl.ANY)
+    pair = pltpu.SemaphoreType.DMA
+    return pl.pallas_call(
+        functools.partial(kernel, n_locus, n_design),
+        out_shape=jax.ShapeDtypeStruct((wins, width), f32),
+        in_specs=[whole, whole, whole, whole, anywhere, anywhere, anywhere, whole],
+        out_specs=whole,
+        scratch_shapes=[
+            pltpu.VMEM((feats, channels), bf16),
+            pltpu.VMEM(dilated_tap_weight.shape, bf16),
+            pltpu.VMEM(mix_weight.shape, bf16),
+            pltpu.VMEM((peers, cap, width // 2), bf16),
+            pltpu.VMEM((peers, 8, 128), f32),
+            pltpu.VMEM((peers, cap, width // 2), bf16),
+            pltpu.VMEM((peers, 8, 128), f32),
+            pltpu.VMEM((blocks + 4, 2, 16, feats), bf16),
+            pltpu.VMEM(((blocks + 4) * 32, channels), bf16),
+            pltpu.VMEM((blocks + 2, 2, 16, own_width), bf16),
+            pltpu.VMEM((tiles, blocks * 16, tile), bf16),
+            pltpu.VMEM((tiles, blocks * 16, tile), bf16),
+            pltpu.VMEM((peers, cap, width // 2), bf16),
+            pltpu.VMEM((peers, cap, width // 2), bf16),
+            pltpu.VMEM((wins, width // 2), bf16),
+            pltpu.VMEM((wins, width // 2), bf16),
+            pair((3,)),
+            pair((2, peers)),
+            pair((2, peers)),
+            pair((2, 1)),
+            pair((2, 1)),
+            pair((2, 4)),
+            pair((2, tiles)),
+            pair((2, peers)),
+            pair((2, 1)),
+        ],
+        compiler_params=pltpu.CompilerParams(
+            collective_id=0, has_side_effects=True, vmem_limit_bytes=60 * 1024 * 1024
+        ),
+    )(
+        base_seq,
+        deltas,
+        owners.reshape(1, wins),
+        slot_ids.reshape(1, wins),
+        stem_weight,
+        dilated_tap_weight,
+        mix_weight,
+        head_weight.reshape(1, channels),
+    )
+
+
+def body(n_locus, n_design, *arrays):
+    base_seq, deltas = arrays[0], arrays[1]
+    wins, width = deltas.shape
+    peers = n_locus * n_design
+    fits = (
+        2 * wins == 32 * peers
+        and wins == 128
+        and width == 512
+        and base_seq.shape[2] == 128
+        and base_seq.shape[1] == 512
+    )
+    if fits:
+        return fused(n_locus, n_design, *arrays)
+    return shards(*arrays)
+
+
 def solution(mesh):
     placed = (
         P(("groups", "design"), "locus", None),
@@ -131,7 +575,7 @@
         P(),
     )
     return jax.shard_map(
-        shards,
+        functools.partial(body, mesh.shape["locus"], mesh.shape["design"]),
         mesh=mesh,
         in_specs=placed,
         out_specs=P(("groups", "locus", "design"), None),

time: 119 us -> 37.8 us (0.32)
  waiting for transfers between devices: 37.1 us -> 0 us
  Pallas kernels: 0 us -> 34.7 us
  blocking collectives: 22.6 us -> 0 us
  starting transfers between devices: 18.2 us -> 0 us
  matrix products: 16 us -> 0 us
  between operations: 13.6 us -> 0.01 us
  other arithmetic: 8.02 us -> 0 us
    pallas_call x0 -> x1, Pallas kernels: none -> 34.7 us  [fused(): pl.pallas_call(functools.partial(kernel, n_locus, n_design), out_shape=ja...]
    psum x1 -> x0, waiting for transfers between devices: 21.2 us -> none  [shards(): summed = lax.psum(part_sum, 'chan')]
    all_to_all x1 -> x0, blocking collectives: 20.5 us -> none  [shards(): lax.all_to_all(back_rows, ('locus', 'design'), split_axis=0, concat_axis=...]
    dot_general x14 -> x0, matrix products: 16 us -> none  [the longest x3 4.77 us: shards(): lax.dot_general(padded_gradient[lower_boundary:lower_boundary + bins_per_...]
    all_to_all x2 -> x0, starting transfers between devices: 10.7 us -> none  [the longest x1 7.25 us: shards(): lax.all_to_all(send_slots, ('locus', 'design'), split_axis=0, concat_axis...]
    all_to_all x2 -> x0, waiting for transfers between devices: 10.3 us -> none  [the longest x1 5.68 us: shards(): lax.all_to_all(send_rows, ('locus', 'design'), split_axis=0, concat_axis=...]
    ppermute x4 -> x0, starting transfers between devices: 7.53 us -> none  [the longest x2 4.95 us: with_halo(): lax.ppermute(tail, axis, [(i, (i + 1) % count) for i in range(ends)])]
    ppermute x4 -> x0, waiting for transfers between devices: 5.54 us -> none  [the longest x2 5.54 us: with_halo(): lax.ppermute(head, axis, [((i + 1) % count, i) for i in range(ends)])]
  transfers between devices with their start and end apart: 7 -> 0, of which waited for: 5 -> 0; matrix products, arithmetic and copies ran while one was open for 5% -> 0% of each run, Pallas kernels for 0% -> 0%
where the time goes in v1:
time: 37.8 us; the launch traced here: 37.7 us
  Pallas kernels  34.7 us (92%)
  local copies, waits for them, and re-layouts  2.96 us (8%)
    pallas_call x1, Pallas kernels, fused(): pl.pallas_call(functools.partial(kernel, n_locus, n_design), out_shape=ja...  34.7 us
    unnamed x1, local copies, waits for them, and re-layouts  1.67 us
    reshape x1, local copies, waits for them, and re-layouts, fused(): head_weight.reshape(1, channels)  1.28 us

profile of v1, /device:TPU:0, one launch (start us, length us, event | category | flops | bytes accessed | tf_op | source)
XLA Modules:
  0.0 37.7 jit_solution(13459351477862769141)
XLA Ops:
  0.0 1.3 %reshape.11.head_ref = bf16[1,1536]{1,0:T(2,128)(2,1)} reshape(bf16[1536]{0:T(1024)(128)(2,1)} %param.15) | data formatting | bytes 6144 | tf_op jit(solution)/shard_map/reshape | solution.py:546
  1.3 34.7 %shard_map.82 = f32[128,512]{1,0:T(8,128)} custom-call(bf16[1,512,128]{2,1,0:T(8,128)(2,1)} %base_ref.1, bf16[128,512]{1,0:T(8,128)(2,1)} %deltas_ref.1, s32[1,128]{1,0:T(1,128)} %bitcast.2, s32[1,128]{1,0:T(1,128)} %bitcast.3, bf16[128,768]{1,0:T(8,128)(2,1)} %stem_hbm.1, bf16[3,1536,384]{2,1,0:T(8,128)(2,1)} %taps_hbm.1, bf16[384,1536]{1,0:T(8,128)(2,1)} %mix_hbm.1, ...), custom_call_target="tpu_custom_call" | custom-call | tf_op jit(solution)/shard_map/pallas_call | solution.py:503
  36.0 1.7 %copy.10 = f32[128,512]{1,0:T(8,128)} copy(f32[128,512]{1,0:T(8,128)} %shard_map.82) | data formatting | bytes 524288

commit v2 on v1

--- a/solution.py
+++ b/solution.py
@@ -159,18 +159,19 @@
     return half + half * gelu_parts(value)[1]
 
 
-def gelu_slope(value):
+def gelu_both(value):
     square, curve = gelu_parts(value)
     root = 0.7978845608028654
     inner = value * (root + (3.0 * root * 0.044715) * square)
-    return 0.5 * (1.0 + curve) + 0.5 * (1.0 - curve * curve) * inner
+    half = 0.5 * (1.0 + curve)
+    return value * half, half + 0.5 * (1.0 - curve * curve) * inner
 
 
 def kernel(
     n_locus,
     n_design,
-    base_ref,
-    deltas_ref,
+    base_hbm,
+    deltas_hbm,
     owners_ref,
     slots_ref,
     stem_hbm,
@@ -178,6 +179,8 @@
     mix_hbm,
     head_ref,
     out_ref,
+    base_ref,
+    deltas_ref,
     stem_ref,
     taps_ref,
     mix_ref,
@@ -187,6 +190,7 @@
     recv_slots,
     seq_ref,
     hidden_ref,
+    slope_ref,
     branch_ref,
     part_send,
     part_recv,
@@ -230,27 +234,30 @@
     load_taps = pltpu.make_async_copy(taps_hbm, taps_ref, load_sem.at[0])
     load_mix = pltpu.make_async_copy(mix_hbm, mix_ref, load_sem.at[1])
     load_stem = pltpu.make_async_copy(stem_hbm, stem_ref.at[:, own_stem], load_sem.at[2])
+    load_base = pltpu.make_async_copy(base_hbm, base_ref, load_sem.at[3])
+    load_deltas = pltpu.make_async_copy(deltas_hbm, deltas_ref, load_sem.at[4])
+    barrier = pltpu.get_barrier_semaphore()
+
+    def greet(device):
+        pl.semaphore_signal(barrier, inc=1, device_id=device, device_id_type=MESH)
+
+    for step in range(1, peers):
+        greet(peer((me + step) % peers))
+    greet(partner)
+
+    @pl.when(locus > 0)
+    def _():
+        greet((group, locus - 1, design, mates))
+
+    @pl.when(locus < n_locus - 1)
+    def _():
+        greet((group, locus + 1, design, mates))
+
+    load_deltas.start()
+    load_base.start()
     load_stem.start()
     load_mix.start()
     load_taps.start()
-
-    barrier = pltpu.get_barrier_semaphore()
-
-    def greet(device):
-        pl.semaphore_signal(barrier, inc=1, device_id=device, device_id_type=MESH)
-
-    for step in range(1, peers):
-        greet(peer((me + step) % peers))
-    greet(partner)
-
-    @pl.when(locus > 0)
-    def _():
-        greet((group, locus - 1, design, mates))
-
-    @pl.when(locus < n_locus - 1)
-    def _():
-        greet((group, locus + 1, design, mates))
-
     bucket_row = owners_ref[...] - me
     bucket_row = jnp.where(bucket_row < 0, bucket_row + peers, bucket_row)
     member = (iota((peers, wins), 0) == bucket_row).astype(jnp.float32)
@@ -259,6 +266,7 @@
     rank_row = jnp.sum(earlier * member, axis=0, keepdims=True).astype(jnp.int32)
     place_row = bucket_row * cap + rank_row
     placer = (iota((peers * cap, wins), 0) == place_row).astype(jnp.bfloat16)
+    load_deltas.wait()
     picked = dot(placer, deltas_ref[:, own_columns]).astype(jnp.bfloat16)
     send_rows[...] = picked.reshape(peers, cap, half_width)
     lane_row = jnp.bitwise_and(place_row, 127)
@@ -282,7 +290,8 @@
         )
 
     row_copies, slot_copies = [], []
-    for step in range(1, peers):
+    far_first = sorted(range(1, peers), key=lambda step: abs(2 * step - peers))
+    for step in far_first:
         device = peer((me + step) % peers)
         slot_copies.append(
             remote(send_slots.at[step], recv_slots.at[step], slots_sem, step, device)
@@ -308,13 +317,14 @@
     line = iota((64, 128), 0)
     wanted = (line // 16) * 32 + (line % 8) * 4 + core * 2 + (line // 8) % 2
     shuffle = (wanted == iota((64, 128), 1)).astype(jnp.bfloat16)
+    load_base.wait()
     base_own = jnp.concatenate(
         [dot(shuffle, base_ref[0, 128 * part : 128 * part + 128, :]) for part in range(blocks // 4)],
         axis=0,
     )
     load_mix.wait()
-    head_row = head_ref[...]
-    mix_grad = dot_nt(jnp.broadcast_to(head_row, (16, channels)), mix_ref[...])[0:1, :]
+    head_row = head_ref[...].astype(jnp.float32).reshape(1, channels)
+    mix_grad = dot_nt(jnp.broadcast_to(head_row, (16, channels)).astype(jnp.bfloat16), mix_ref[...])[0:1, :]
 
     for copy in slot_copies:
         copy.wait_recv()
@@ -371,8 +381,22 @@
     seq_copy.start()
     load_stem.wait()
     stem_copy.wait()
-    load_taps.wait()
+    own_rows = blocks * 16
+    for part in range(tiles):
+        columns = slice(part * tile, part * tile + tile)
+        pre_act = dot(seq_own, stem_ref[:, columns])
+        value, slope_ref[:, columns] = gelu_both(pre_act)
+        hidden_ref[pl.ds(2, blocks), core, :, columns] = value.astype(jnp.bfloat16).reshape(
+            blocks, 16, tile
+        )
     seq_copy.wait()
+    seq_mate = seq_ref[pl.ds(2, blocks), mates].reshape(own_rows, 128)
+    for part in range(tiles):
+        columns = slice(part * tile, part * tile + tile)
+        pre_act = dot(seq_mate, stem_ref[:, columns])
+        hidden_ref[pl.ds(2, blocks), mates, :, columns] = (
+            gelu_value(pre_act).astype(jnp.bfloat16).reshape(blocks, 16, tile)
+        )
 
     @pl.when(locus > 0)
     def _():
@@ -384,17 +408,22 @@
         for copy in down:
             copy.wait_recv()
 
-    rows_all = (blocks + 4) * 32
-    conv_rows = (blocks + 2) * 32
-    seq_all = seq_ref[...].reshape(rows_all, 128)
+    seq_edges = jnp.concatenate(
+        [seq_ref[0:2].reshape(64, 128), seq_ref[blocks + 2 : blocks + 4].reshape(64, 128)], axis=0
+    )
     for part in range(tiles):
         columns = slice(part * tile, part * tile + tile)
-        pre_act = dot(seq_all, stem_ref[:, columns])
-        hidden_ref[:, columns] = gelu_value(pre_act).astype(jnp.bfloat16)
-
-    conv = dot(hidden_ref[0:conv_rows, :], taps_ref[0])
-    for tap in range(1, 3):
-        conv = conv + dot(hidden_ref[32 * tap : 32 * tap + conv_rows, :], taps_ref[tap])
+        value = gelu_value(dot(seq_edges, stem_ref[:, columns])).astype(jnp.bfloat16)
+        value = value.reshape(4, 2, 16, tile)
+        hidden_ref[0:2, :, :, columns] = value[0:2]
+        hidden_ref[blocks + 2 : blocks + 4, :, :, columns] = value[2:4]
+
+    conv_blocks = blocks + 2
+    load_taps.wait()
+    conv = jnp.zeros((conv_blocks * 32, taps_ref.shape[2]), jnp.float32)
+    for tap in range(3):
+        rows = hidden_ref[tap : tap + conv_blocks].reshape(conv_blocks * 32, channels)
+        conv = conv + dot(rows, taps_ref[tap])
     branch = (silu_slope(conv) * mix_grad).astype(jnp.bfloat16)
     branch_ref[...] = branch.reshape(branch_ref.shape)
 
@@ -405,8 +434,6 @@
     @pl.when(locus == n_locus - 1)
     def _():
         branch_ref[blocks + 1] = jnp.zeros(branch_ref.shape[1:], jnp.bfloat16)
-
-    own_rows = blocks * 16
 
     def taps_of(side):
         return [
@@ -433,10 +460,9 @@
     seq_grad = jnp.zeros((own_rows, 128), jnp.float32)
     for part in range(tiles):
         columns = slice(part * tile, part * tile + tile)
-        own = back_tile(ours, part) + head_row[:, columns].astype(jnp.float32)
-        slope = gelu_slope(dot(seq_own, stem_ref[:, columns]))
+        own = back_tile(ours, part) + head_row[:, columns]
         part_copies[part].wait_recv()
-        pulled = slope * (own + part_recv[part].astype(jnp.float32))
+        pulled = slope_ref[:, columns] * (own + part_recv[part].astype(jnp.float32))
         seq_grad = seq_grad + dot_nt(pulled.astype(jnp.bfloat16), stem_ref[:, columns])
 
     grads = seq_grad.reshape(blocks, 2, 8, 128)
@@ -446,7 +472,7 @@
     back = dot(chooser, slot_grad).astype(jnp.bfloat16)
     back_ref[...] = back.reshape(back_ref.shape)
     back_copies = []
-    for step in range(1, peers):
+    for step in far_first:
         device = peer((me + peers - step) % peers)
         back_copies.append(remote(back_ref.at[step], ret_ref.at[step], back_sem, step, device))
         back_copies[-1].start()
@@ -455,7 +481,8 @@
     for copy in back_copies:
         copy.wait_recv()
     result = dot(unplacer, ret_ref[...].reshape(peers * cap, half_width))
-    half_ref[...] = result.astype(jnp.bfloat16)
+    result = result.astype(jnp.bfloat16)
+    half_ref[...] = result
     half_copy = remote(half_ref, other_ref, half_sem, 0, partner)
     half_copy.start()
     out_ref[:, own_columns] = result
@@ -473,7 +500,7 @@
             copy.wait_send()
 
     half_copy.wait()
-    out_ref[:, other_columns] = other_ref[...].astype(jnp.float32)
+    out_ref[:, other_columns] = other_ref[...]
 
 
 def fused(
@@ -502,10 +529,12 @@
     pair = pltpu.SemaphoreType.DMA
     return pl.pallas_call(
         functools.partial(kernel, n_locus, n_design),
-        out_shape=jax.ShapeDtypeStruct((wins, width), f32),
-        in_specs=[whole, whole, whole, whole, anywhere, anywhere, anywhere, whole],
+        out_shape=jax.ShapeDtypeStruct((wins, width), bf16),
+        in_specs=[anywhere, anywhere, whole, whole, anywhere, anywhere, anywhere, whole],
         out_specs=whole,
         scratch_shapes=[
+            pltpu.VMEM(base_seq.shape, bf16),
+            pltpu.VMEM(deltas.shape, bf16),
             pltpu.VMEM((feats, channels), bf16),
             pltpu.VMEM(dilated_tap_weight.shape, bf16),
             pltpu.VMEM(mix_weight.shape, bf16),
@@ -514,7 +543,8 @@
             pltpu.VMEM((peers, cap, width // 2), bf16),
             pltpu.VMEM((peers, 8, 128), f32),
             pltpu.VMEM((blocks + 4, 2, 16, feats), bf16),
-            pltpu.VMEM(((blocks + 4) * 32, channels), bf16),
+            pltpu.VMEM((blocks + 4, 2, 16, channels), bf16),
+            pltpu.VMEM((blocks * 16, channels), f32),
             pltpu.VMEM((blocks + 2, 2, 16, own_width), bf16),
             pltpu.VMEM((tiles, blocks * 16, tile), bf16),
             pltpu.VMEM((tiles, blocks * 16, tile), bf16),
@@ -522,7 +552,7 @@
             pltpu.VMEM((peers, cap, width // 2), bf16),
             pltpu.VMEM((wins, width // 2), bf16),
             pltpu.VMEM((wins, width // 2), bf16),
-            pair((3,)),
+            pair((5,)),
             pair((2, peers)),
             pair((2, peers)),
             pair((2, 1)),
@@ -543,8 +573,8 @@
         stem_weight,
         dilated_tap_weight,
         mix_weight,
-        head_weight.reshape(1, channels),
-    )
+        head_weight,
+    ).astype(f32)
 
 
 def body(n_locus, n_design, *arrays):

time: 37.8 us -> 35.5 us (0.939)
  local copies, waits for them, and re-layouts: 2.96 us -> 0 us
  other arithmetic: 0 us -> 1.63 us
  Pallas kernels: 34.7 us -> 33.6 us
    unnamed x1 -> x0, local copies, waits for them, and re-layouts: 1.67 us -> none
    convert_element_type x0 -> x1, other arithmetic: none -> 1.63 us  [fused(): return pl.pallas_call(functools.partial(kernel, n_locus, n_design), out_s...]
    reshape x1 -> x0, local copies, waits for them, and re-layouts: 1.28 us -> none  [fused(): head_weight.reshape(1, channels)]
    pallas_call x1, Pallas kernels: 34.7 us -> 33.6 us  [fused(): pl.pallas_call(functools.partial(kernel, n_locus, n_design), out_shape=ja...]
where the time goes in v2:
time: 35.5 us; the launch traced here: 35.3 us
  Pallas kernels  33.6 us (95%)
  other arithmetic  1.63 us (5%)
    pallas_call x1, Pallas kernels, fused(): pl.pallas_call(functools.partial(kernel, n_locus, n_design), out_shape=ja...  33.6 us
    convert_element_type x1, other arithmetic, fused(): return pl.pallas_call(functools.partial(kernel, n_locus, n_design), out_s...  1.63 us

profile of v2, /device:TPU:0, one launch (start us, length us, event | category | flops | bytes accessed | tf_op | source)
XLA Modules:
  0.0 35.3 jit_solution(2524887826780553901)
XLA Ops:
  0.0 33.6 %shard_map.82 = bf16[128,512]{1,0:T(8,128)(2,1)} custom-call(bf16[1,512,128]{2,1,0:T(8,128)(2,1)} %base_hbm.1, bf16[128,512]{1,0:T(8,128)(2,1)} %deltas_hbm.1, s32[1,128]{1,0:T(1,128)} %bitcast.2, s32[1,128]{1,0:T(1,128)} %bitcast.3, bf16[128,768]{1,0:T(8,128)(2,1)} %stem_hbm.1, bf16[3,1536,384]{2,1,0:T(8,128)(2,1)} %taps_hbm.1, bf16[384,1536]{1,0:T(8,128)(2,1)} %mix_hbm.1, ...), custom_call_target="tpu_custom_call" | custom-call | tf_op jit(solution)/shard_map/pallas_call | solution.py:530
  33.6 1.6 %convert_element_type.3 = f32[128,512]{1,0:T(8,128)} convert(bf16[128,512]{1,0:T(8,128)(2,1)} %shard_map.82) | non-fusion elementwise | flops 65536 | bytes 393216 | tf_op jit(solution)/shard_map/convert_element_type | solution.py:577

commit v3 on v2

--- a/solution.py
+++ b/solution.py
@@ -420,20 +420,23 @@
 
     conv_blocks = blocks + 2
     load_taps.wait()
-    conv = jnp.zeros((conv_blocks * 32, taps_ref.shape[2]), jnp.float32)
-    for tap in range(3):
-        rows = hidden_ref[tap : tap + conv_blocks].reshape(conv_blocks * 32, channels)
-        conv = conv + dot(rows, taps_ref[tap])
-    branch = (silu_slope(conv) * mix_grad).astype(jnp.bfloat16)
-    branch_ref[...] = branch.reshape(branch_ref.shape)
-
-    @pl.when(locus == 0)
-    def _():
-        branch_ref[0] = jnp.zeros(branch_ref.shape[1:], jnp.bfloat16)
-
-    @pl.when(locus == n_locus - 1)
-    def _():
-        branch_ref[blocks + 1] = jnp.zeros(branch_ref.shape[1:], jnp.bfloat16)
+
+    def branch_of(side):
+        conv = jnp.zeros((conv_blocks * 16, taps_ref.shape[2]), jnp.float32)
+        for tap in range(3):
+            rows = hidden_ref[tap : tap + conv_blocks, side].reshape(conv_blocks * 16, channels)
+            conv = conv + dot(rows, taps_ref[tap])
+        branch = (silu_slope(conv) * mix_grad).astype(jnp.bfloat16)
+        branch_ref[:, side] = branch.reshape(conv_blocks, 16, taps_ref.shape[2])
+        nothing = jnp.zeros((16, taps_ref.shape[2]), jnp.bfloat16)
+
+        @pl.when(locus == 0)
+        def _():
+            branch_ref[0, side] = nothing
+
+        @pl.when(locus == n_locus - 1)
+        def _():
+            branch_ref[blocks + 1, side] = nothing
 
     def taps_of(side):
         return [
@@ -448,6 +451,7 @@
             total = total + dot_nt(inputs[tap], taps_ref[tap, lines, :])
         return total
 
+    branch_of(mates)
     theirs = taps_of(mates)
     part_copies = []
     for part in range(tiles):
@@ -456,6 +460,7 @@
             remote(part_send.at[part], part_recv.at[part], part_sem, part, partner)
         )
         part_copies[-1].start()
+    branch_of(core)
     ours = taps_of(core)
     seq_grad = jnp.zeros((own_rows, 128), jnp.float32)
     for part in range(tiles):

time: 35.5 us -> 35.6 us (level)
  no operation moved by 1% of the time
where the time goes in v3:
time: 35.6 us; the launch traced here: 35.4 us
  Pallas kernels  33.8 us (95%)
  other arithmetic  1.63 us (5%)
    pallas_call x1, Pallas kernels, fused(): pl.pallas_call(functools.partial(kernel, n_locus, n_design), out_shape=ja...  33.8 us
    convert_element_type x1, other arithmetic, fused(): return pl.pallas_call(functools.partial(kernel, n_locus, n_design), out_s...  1.63 us

profile of v3, /device:TPU:0, one launch (start us, length us, event | category | flops | bytes accessed | tf_op | source)
XLA Modules:
  0.0 35.4 jit_solution(14167602387487384904)
XLA Ops:
  0.0 33.8 %shard_map.82 = bf16[128,512]{1,0:T(8,128)(2,1)} custom-call(bf16[1,512,128]{2,1,0:T(8,128)(2,1)} %base_hbm.1, bf16[128,512]{1,0:T(8,128)(2,1)} %deltas_hbm.1, s32[1,128]{1,0:T(1,128)} %bitcast.2, s32[1,128]{1,0:T(1,128)} %bitcast.3, bf16[128,768]{1,0:T(8,128)(2,1)} %stem_hbm.1, bf16[3,1536,384]{2,1,0:T(8,128)(2,1)} %taps_hbm.1, bf16[384,1536]{1,0:T(8,128)(2,1)} %mix_hbm.1, ...), custom_call_target="tpu_custom_call" | custom-call | tf_op jit(solution)/shard_map/pallas_call | solution.py:535
  33.8 1.6 %convert_element_type.3 = f32[128,512]{1,0:T(8,128)} convert(bf16[128,512]{1,0:T(8,128)(2,1)} %shard_map.82) | non-fusion elementwise | flops 65536 | bytes 393216 | tf_op jit(solution)/shard_map/convert_element_type | solution.py:582

commit v4 on v2

--- a/solution.py
+++ b/solution.py
@@ -448,22 +448,26 @@
             total = total + dot_nt(inputs[tap], taps_ref[tap, lines, :])
         return total
 
-    theirs = taps_of(mates)
-    part_copies = []
-    for part in range(tiles):
-        part_send[part] = back_tile(theirs, part).astype(jnp.bfloat16)
-        part_copies.append(
-            remote(part_send.at[part], part_recv.at[part], part_sem, part, partner)
-        )
-        part_copies[-1].start()
-    ours = taps_of(core)
+    both = [jnp.concatenate(pair, axis=0) for pair in zip(taps_of(mates), taps_of(core))]
+    part_copies, kept = [], []
     seq_grad = jnp.zeros((own_rows, 128), jnp.float32)
-    for part in range(tiles):
-        columns = slice(part * tile, part * tile + tile)
-        own = back_tile(ours, part) + head_row[:, columns]
-        part_copies[part].wait_recv()
-        pulled = slope_ref[:, columns] * (own + part_recv[part].astype(jnp.float32))
-        seq_grad = seq_grad + dot_nt(pulled.astype(jnp.bfloat16), stem_ref[:, columns])
+    lag = 3
+    for part in range(tiles + lag):
+        if part < tiles:
+            terms = back_tile(both, part)
+            part_send[part] = terms[0:own_rows].astype(jnp.bfloat16)
+            part_copies.append(
+                remote(part_send.at[part], part_recv.at[part], part_sem, part, partner)
+            )
+            part_copies[-1].start()
+            kept.append(terms[own_rows:])
+        if part >= lag:
+            done = part - lag
+            columns = slice(done * tile, done * tile + tile)
+            own = kept[done] + head_row[:, columns]
+            part_copies[done].wait_recv()
+            pulled = slope_ref[:, columns] * (own + part_recv[done].astype(jnp.float32))
+            seq_grad = seq_grad + dot_nt(pulled.astype(jnp.bfloat16), stem_ref[:, columns])
 
     grads = seq_grad.reshape(blocks, 2, 8, 128)
     slot_grad = jnp.concatenate(

time: 35.5 us -> 35.2 us (level)
  no operation moved by 1% of the time
where the time goes in v4:
time: 35.2 us; the launch traced here: 35 us
  Pallas kernels  33.4 us (95%)
  other arithmetic  1.63 us (5%)
    pallas_call x1, Pallas kernels, fused(): pl.pallas_call(functools.partial(kernel, n_locus, n_design), out_shape=ja...  33.4 us
    convert_element_type x1, other arithmetic, fused(): return pl.pallas_call(functools.partial(kernel, n_locus, n_design), out_s...  1.63 us

profile of v4, /device:TPU:0, one launch (start us, length us, event | category | flops | bytes accessed | tf_op | source)
XLA Modules:
  0.0 35.0 jit_solution(14282622043183887609)
XLA Ops:
  0.0 33.4 %shard_map.82 = bf16[128,512]{1,0:T(8,128)(2,1)} custom-call(bf16[1,512,128]{2,1,0:T(8,128)(2,1)} %base_hbm.1, bf16[128,512]{1,0:T(8,128)(2,1)} %deltas_hbm.1, s32[1,128]{1,0:T(1,128)} %bitcast.2, s32[1,128]{1,0:T(1,128)} %bitcast.3, bf16[128,768]{1,0:T(8,128)(2,1)} %stem_hbm.1, bf16[3,1536,384]{2,1,0:T(8,128)(2,1)} %taps_hbm.1, bf16[384,1536]{1,0:T(8,128)(2,1)} %mix_hbm.1, ...), custom_call_target="tpu_custom_call" | custom-call | tf_op jit(solution)/shard_map/pallas_call | solution.py:534
  33.4 1.6 %convert_element_type.3 = f32[128,512]{1,0:T(8,128)} convert(bf16[128,512]{1,0:T(8,128)(2,1)} %shard_map.82) | non-fusion elementwise | flops 65536 | bytes 393216 | tf_op jit(solution)/shard_map/convert_element_type | solution.py:581
